TPU v7x, 32 devices: a whole 2x2x4 slice. The times are simulated.
32 devices in a mesh: grp: 2 (over y), ew: 4 (over z), ns: 2 (over x), lvl: 2 (over core).
Axes of the slice: x: 2, y: 2, z: 4, core: 2. Of those that a mesh axis runs over, the one named last changes fastest.
Arguments:
- probe_fine: int32 [8, 128, 512], P('lvl', 'ew', 'ns'), may hold values from 0 to 1
- probe_coarse: int32 [8, 64, 256], P('lvl', 'ew', 'ns'), may hold values from 0 to 1
- kappa_fine: float32 [256, 512], P(('grp', 'ew'), 'ns'), parts along dimension 0, may hold values from 0.2 to 2
- kappa_coarse: float32 [128, 256], P(('grp', 'ew'), 'ns'), parts along dimension 0, may hold values from 0.2 to 2
- phi_tiles: float32 [1024, 128, 128], P(('ew', 'ns')), may hold values from -0.5 to 0.5
- obs_weight: float32 [2048, 128], P(('grp', 'ew', 'ns')), parts along dimension 0, may hold values from 4 to 40
- block_index: int32 [1024], P(('ew', 'ns')), may hold values from 0 to 85, as said below
- block_count: int32 [8], P(('ew', 'ns')), may hold values from 2 to 128, as said below
Outputs:
- solve_fine: float32 [16, 128, 512], P(('grp', 'lvl'), 'ew', 'ns'), parts along dimension 0
- solve_coarse: float32 [16, 64, 256], P(('grp', 'lvl'), 'ew', 'ns'), parts along dimension 0
- resid_fine: float32 [16, 128, 512], P(('grp', 'lvl'), 'ew', 'ns'), parts along dimension 0
- resid_coarse: float32 [16, 64, 256], P(('grp', 'lvl'), 'ew', 'ns'), parts along dimension 0
There are 2 independent parts, one for each index of `grp`. A program takes and returns all parts, laid end to end along the dimension named above; an argument that names none is the same for every part. Nothing has to cross between parts.
Inputs may be any that keep to these rules, and one draw needn't show every extreme that they name: `block_count`: every device has 2 or more live blocks, and only blocks below its count carry observations; some device has all 128 slots live. `block_index`: A block's tile is one of its own device's 86 tiles, in the order of the tile list; each device's first block names a tile of its western outside row (fine or coarse) and its second block a tile of its eastern outside row.
All inputs are finite; a program needn't handle non-finite values.
Results may differ from a plain program's by a relative error of at most 0.0003.
Values sent between devices are 32-bit elements; how exact they have to be, the bound alone decides.
A program may use at most 64 MiB of HBM per device.

v0:
```python
import jax
import jax.numpy as jnp
from jax import lax
from jax.sharding import PartitionSpec as P

ITERS = 2


def with_halo(block, sides, width):
    for axis, dim in sides:
        count = lax.axis_size(axis)
        forward = [(i, i + 1) for i in range(count - 1)]
        backward = [(target, source) for source, target in forward]
        low = lax.ppermute(
            lax.slice_in_dim(block, block.shape[dim] - width, None, axis=dim), axis, forward
        )
        high = lax.ppermute(lax.slice_in_dim(block, 0, width, axis=dim), axis, backward)
        block = jnp.concatenate([low, block, high], axis=dim)
    return block


def shifted(block, axis, distance):
    devices = range(lax.axis_size(axis))
    route = [(i - distance, i) for i in devices if i - distance in devices]
    return lax.ppermute(block, axis, route)


def apply_sar(padded, kappa):
    centre = padded[:, 1:-1, 1:-1]
    beside_all = (
        padded[:, 2:, 1:-1] + padded[:, :-2, 1:-1] + padded[:, 1:-1, 2:] + padded[:, 1:-1, :-2]
    )
    return (4.0 + kappa) * centre - beside_all


def fine_faces(field):
    return with_halo(field, (("ew", 1), ("ns", 2)), 1)


def coarse_faces(field):
    return with_halo(field, (("ew", 1), ("ns", 2)), 1)


def local_products(first_fine, first_coarse, second_fine, second_coarse):
    return jnp.sum(first_fine * second_fine, axis=(1, 2)) + jnp.sum(
        first_coarse * second_coarse, axis=(1, 2)
    )


def local(
    probe_fine,
    probe_coarse,
    kappa_fine,
    kappa_coarse,
    phi_tiles,
    obs_weight,
    block_index,
    block_count,
):
    probes, rows, width = probe_fine.shape
    half_rows = probe_coarse.shape[1]
    tile = phi_tiles.shape[1]
    blocks = phi_tiles.shape[0]
    fine_count = (rows + 2) * (width // tile)
    tile_total = fine_count + half_rows + 2
    live = (jnp.arange(blocks, dtype=jnp.int32) < block_count[0]).astype(jnp.float32)
    weights = (obs_weight * live[:, None])[None]
    onehot = (block_index[:, None] == jnp.arange(tile_total, dtype=jnp.int32)[None, :]).astype(
        jnp.float32
    )
    resid_fine = (2 * probe_fine - 1).astype(jnp.float32)
    resid_coarse = (2 * probe_coarse - 1).astype(jnp.float32)
    solve_fine = jnp.zeros_like(resid_fine)
    solve_coarse = jnp.zeros_like(resid_coarse)

    def squares(first_fine, first_coarse):
        return lax.psum(
            local_products(first_fine, first_coarse, first_fine, first_coarse), ("ew", "ns")
        )

    direction_fine, direction_coarse = (resid_fine, resid_coarse)
    norm_now = squares(resid_fine, resid_coarse)
    for iteration in range(ITERS):
        halo_fine = fine_faces(direction_fine)
        halo_coarse = coarse_faces(direction_coarse)
        prior_fine = apply_sar(fine_faces(apply_sar(halo_fine, kappa_fine)), kappa_fine)
        prior_coarse = apply_sar(coarse_faces(apply_sar(halo_coarse, kappa_coarse)), kappa_coarse)
        rows_fine = halo_fine[:, :, 1:-1]
        rows_coarse = halo_coarse[:, :, 1:-1]
        ext = jnp.concatenate([rows_fine.reshape(probes, fine_count, tile), rows_coarse], axis=1)
        picked = jnp.take(ext, block_index, axis=1)
        seen = jnp.einsum(
            "bij,pbj->pbi",
            phi_tiles,
            picked,
            precision=lax.Precision.HIGHEST,
            preferred_element_type=jnp.float32,
        )
        scaled = seen * weights
        back = jnp.einsum(
            "bij,pbi->pbj",
            phi_tiles,
            scaled,
            precision=lax.Precision.HIGHEST,
            preferred_element_type=jnp.float32,
        )
        adjoint = jnp.einsum("pbj,bt->ptj", back, onehot, precision=lax.Precision.HIGHEST)
        adj_fine = adjoint[:, :fine_count].reshape(probes, rows + 2, width)
        adj_coarse = adjoint[:, fine_count:]
        west_row = jnp.concatenate([adj_fine[:, 0], adj_coarse[:, 0]], axis=-1)
        east_row = jnp.concatenate([adj_fine[:, -1], adj_coarse[:, -1]], axis=-1)
        from_next = shifted(west_row, "ew", -1)
        from_prev = shifted(east_row, "ew", 1)
        inner_fine = adj_fine[:, 1:-1]
        inner_fine = (
            inner_fine.at[:, 0].add(from_prev[:, :width]).at[:, -1].add(from_next[:, :width])
        )
        inner_coarse = adj_coarse[:, 1:-1]
        inner_coarse = (
            inner_coarse.at[:, 0].add(from_prev[:, width:]).at[:, -1].add(from_next[:, width:])
        )
        image_fine = prior_fine + inner_fine
        image_coarse = prior_coarse + inner_coarse
        curve = lax.psum(
            local_products(direction_fine, direction_coarse, image_fine, image_coarse), ("ew", "ns")
        )
        alpha = (norm_now / curve)[:, None, None]
        solve_fine = solve_fine + alpha * direction_fine
        solve_coarse = solve_coarse + alpha * direction_coarse
        resid_fine = resid_fine - alpha * image_fine
        resid_coarse = resid_coarse - alpha * image_coarse
        if iteration + 1 < ITERS:
            norm_next = squares(resid_fine, resid_coarse)
            ratio = (norm_next / norm_now)[:, None, None]
            direction_fine = resid_fine + ratio * direction_fine
            direction_coarse = resid_coarse + ratio * direction_coarse
            norm_now = norm_next
    return (solve_fine, solve_coarse, resid_fine, resid_coarse)


def solution(mesh):
    in_specs = (
        P("lvl", "ew", "ns"),
        P("lvl", "ew", "ns"),
        P(("grp", "ew"), "ns"),
        P(("grp", "ew"), "ns"),
        P(("ew", "ns"), None, None),
        P(("grp", "ew", "ns"), None),
        P(("ew", "ns")),
        P(("ew", "ns")),
    )
    out_specs = (
        P(("grp", "lvl"), "ew", "ns"),
        P(("grp", "lvl"), "ew", "ns"),
        P(("grp", "lvl"), "ew", "ns"),
        P(("grp", "lvl"), "ew", "ns"),
    )
    return jax.shard_map(local, mesh=mesh, in_specs=in_specs, out_specs=out_specs, check_vma=False)
```

profile of v0, /device:TPU:0, one launch (start us, length us, event | category | flops | bytes accessed | tf_op | source)
XLA Modules:
  0.0 239.9 jit_solution(14725809653699780462)
XLA Ops:
  0.6 0.8 add_convert_fusion
  1.4 1.3 collective-permute-start.9
  2.7 5.6 %collective-permute-start.8 = (f32[4,1,128]{2,1,0:T(1,128)S(1)}, f32[4,1,128]{2,1,0:T(1,128)S(1)}, u32[]{:S(2)}, u32[]{:S(2)}) collective-permute-start(f32[4,1,128]{2,1,0:T(1,128)S(1)} %get-tuple-element.164), channel_id=1, source_target_pairs={{0,4},{4,8},{8,12},{1,5},{5,9},{9,13},{2,6},{6,10},{10,14},{3,7},{... | collective-permute-start | bytes 6152 | tf_op jit(solution)/shard_map/ppermute | solution.py:14
  8.3 1.0 fusion.30
  9.3 1.3 collective-permute-start
  10.6 4.6 %collective-permute-start.1 = (f32[4,1,256]{2,0,1:T(4,128)S(1)}, f32[4,1,256]{2,0,1:T(4,128)S(1)}, u32[]{:S(2)}, u32[]{:S(2)}) collective-permute-start(f32[4,1,256]{2,0,1:T(4,128)S(1)} %get-tuple-element.146), channel_id=1, source_target_pairs={{0,4},{4,8},{8,12},{1,5},{5,9},{9,13},{2,6},{6,10},{10,14},{3,7},{... | collective-permute-start | bytes 12296 | tf_op jit(solution)/shard_map/ppermute | solution.py:14
  15.2 0.7 compare_select_fusion
  16.5 0.8 broadcast_add_fusion
  17.2 0.7 broadcast_add_fusion.1
  17.9 0.9 broadcast_multiply_fusion
  18.9 0.7 compare_and_fusion
  19.6 3.8 %collective-permute-start.13 = (f32[4,18,1]{2,1,0:T(8,128)S(1)}, f32[4,18,1]{2,1,0:T(8,128)S(1)}, u32[]{:S(2)}, u32[]{:S(2)}) collective-permute-start(f32[4,18,1]{2,1,0:T(8,128)S(1)} %get-tuple-element.155), channel_id=1, source_target_pairs={{0,2},{1,3},{4,6},{5,7},{8,10},{9,11},{12,14},{13,15},{16,18},{17,... | collective-permute-start | bytes 872 | tf_op jit(solution)/shard_map/ppermute | solution.py:14
  23.5 1.3 collective-permute-start.12
  24.8 0.4 collective-permute-done.13
  25.2 4.3 %collective-permute-done.12 = f32[4,18,1]{2,1,0:T(8,128)S(1)} collective-permute-done((f32[4,18,1]{2,1,0:T(8,128)S(1)}, f32[4,18,1]{2,1,0:T(8,128)S(1)}, u32[]{:S(2)}, u32[]{:S(2)}) %collective-permute-start.12) | collective-permute-done | bytes 320 | tf_op jit(solution)/shard_map/ppermute | solution.py:17
  29.6 1.3 collective-permute-start.14
  30.9 4.5 %collective-permute-start.15 = (f32[4,1,128]{2,1,0:T(1,128)S(1)}, f32[4,1,128]{2,1,0:T(1,128)S(1)}, u32[]{:S(2)}, u32[]{:S(2)}) collective-permute-start(f32[4,1,128]{2,1,0:T(1,128)S(1)} %get-tuple-element.162), channel_id=1, source_target_pairs={{0,4},{4,8},{8,12},{1,5},{5,9},{9,13},{2,6},{6,10},{10,14},{3,7},{... | collective-permute-start | bytes 6152 | tf_op jit(solution)/shard_map/ppermute | solution.py:14
  35.5 0.8 gather_fusion
  36.3 16.4 %fusion.1 = f32[4,128,128]{2,0,1:T(4,128)S(1)} fusion(f32[128,128,128]{2,1,0:T(8,128)} %param.30, f32[128,4,128]{2,1,0:T(4,128)S(1)} %gather_fusion, f32[128,128]{1,0:T(8,128)S(1)} %broadcast_multiply_fusion, pred[128]{0:T(512)(128)(4,1)S(1)} %compare_and_fusion), kind=kOutput, calls=%fused_computation.5 | convolution fusion | flops 100794368 | bytes 8978560 | tf_op jit(solution)/shard_map/bij,pbj->pbi/dot_general | solution.py:92
  52.7 7.3 %fusion.92 = f32[128,4,128]{2,1,0:T(4,128)S(1)} fusion(f32[4,128,128]{2,0,1:T(4,128)S(1)} %fusion.1, f32[128,128,128]{2,1,0:T(8,128)S(1)} %copy-done), kind=kOutput, calls=%fused_computation.209 | convolution fusion | flops 100663296 | bytes 8912896 | tf_op jit(solution)/shard_map/bij,pbi->pbj/dot_general | solution.py:100
  60.6 3.5 %collective-permute-start.10 = (f32[4,384]{1,0:T(4,128)S(1)}, f32[4,384]{1,0:T(4,128)S(1)}, u32[]{:S(2)}, u32[]{:S(2)}) collective-permute-start(f32[4,384]{1,0:T(4,128)S(1)} %pad_maximum_fusion.74), channel_id=1, source_target_pairs={{0,4},{4,8},{8,12},{1,5},{5,9},{9,13},{2,6},{6,10},{10,14},{3,7},{... | collective-permute-start | bytes 18440 | tf_op jit(solution)/shard_map/ppermute | solution.py:25
  64.1 1.6 collective-permute-start.3
  65.7 1.5 collective-permute-start.2
  67.3 0.4 collective-permute-done.3
  67.7 4.5 %collective-permute-done.2 = f32[4,34,1]{2,0,1:T(4,128)S(1)} collective-permute-done((f32[4,34,1]{2,0,1:T(4,128)S(1)}, f32[4,34,1]{2,0,1:T(4,128)S(1)}, u32[]{:S(2)}, u32[]{:S(2)}) %collective-permute-start.2) | collective-permute-done | bytes 576 | tf_op jit(solution)/shard_map/ppermute | solution.py:17
  72.4 1.3 collective-permute-start.4
  73.7 4.5 %collective-permute-start.5 = (f32[4,1,256]{2,0,1:T(4,128)S(1)}, f32[4,1,256]{2,0,1:T(4,128)S(1)}, u32[]{:S(2)}, u32[]{:S(2)}) collective-permute-start(f32[4,1,256]{2,0,1:T(4,128)S(1)} %get-tuple-element.144), channel_id=1, source_target_pairs={{0,4},{4,8},{8,12},{1,5},{5,9},{9,13},{2,6},{6,10},{10,14},{3,7},{... | collective-permute-start | bytes 12296 | tf_op jit(solution)/shard_map/ppermute | solution.py:14
  78.3 1.6 collective-permute-start.17
  79.9 1.3 collective-permute-start.16
  81.3 4.5 %collective-permute-start.7 = (f32[4,34,1]{2,0,1:T(4,128)S(1)}, f32[4,34,1]{2,0,1:T(4,128)S(1)}, u32[]{:S(2)}, u32[]{:S(2)}) collective-permute-start(f32[4,34,1]{2,0,1:T(4,128)S(1)} %get-tuple-element.135), channel_id=1, source_target_pairs={{0,2},{1,3},{4,6},{5,7},{8,10},{9,11},{12,14},{13,15},{16,18},{17,... | collective-permute-start | bytes 1640 | tf_op jit(solution)/shard_map/ppermute | solution.py:14
  85.9 1.3 collective-permute-start.6
  87.2 1.3 collective-permute-start.11
  88.6 4.2 %collective-permute-done.11 = f32[4,384]{1,0:T(4,128)S(1)} collective-permute-done((f32[4,384]{1,0:T(4,128)S(1)}, f32[4,384]{1,0:T(4,128)S(1)}, u32[]{:S(2)}, u32[]{:S(2)}) %collective-permute-start.11) | collective-permute-done | bytes 6176 | tf_op jit(solution)/shard_map/ppermute | solution.py:25
  93.5 19.8 %all-reduce = (f32[4]{0:T(128)S(1)}, f32[4]{0:T(128)S(1)}) all-reduce(f32[4]{0:T(128)S(1)} %add.192, f32[4]{0:T(128)S(1)} %add.213), channel_id=1, replica_groups=mesh['grp'=2,'ew'=4,'ns'=2,'lvl'=2] {'ew','ns'}, use_global_device_ids=true, to_apply=%region_2.0 | all-reduce | flops 8 | bytes 64 | tf_op jit(solution)/shard_map/psum | solution.py:77
  113.7 17.3 %psum.30 = f32[4]{0:T(128)S(1)} all-reduce(f32[4]{0:T(128)S(1)} %add.214), channel_id=1, replica_groups=mesh['grp'=2,'ew'=4,'ns'=2,'lvl'=2] {'ew','ns'}, use_global_device_ids=true, to_apply=%region_8.10 | all-reduce | flops 4 | bytes 32 | tf_op jit(solution)/shard_map/psum | solution.py:77
  131.3 1.3 collective-permute-start.27
  132.6 4.5 %collective-permute-start.26 = (f32[4,1,128]{2,1,0:T(1,128)S(1)}, f32[4,1,128]{2,1,0:T(1,128)S(1)}, u32[]{:S(2)}, u32[]{:S(2)}) collective-permute-start(f32[4,1,128]{2,1,0:T(1,128)S(1)} %get-tuple-element.160), channel_id=1, source_target_pairs={{0,4},{4,8},{8,12},{1,5},{5,9},{9,13},{2,6},{6,10},{10,14},{3,7},{... | collective-permute-start | bytes 6152 | tf_op jit(solution)/shard_map/ppermute | solution.py:14
  137.2 1.2 collective-permute-done.26
  138.5 3.7 %collective-permute-start.31 = (f32[4,18,1]{2,1,0:T(8,128)S(1)}, f32[4,18,1]{2,1,0:T(8,128)S(1)}, u32[]{:S(2)}, u32[]{:S(2)}) collective-permute-start(f32[4,18,1]{2,1,0:T(8,128)S(1)} %get-tuple-element.151), channel_id=1, source_target_pairs={{0,2},{1,3},{4,6},{5,7},{8,10},{9,11},{12,14},{13,15},{16,18},{17,... | collective-permute-start | bytes 872 | tf_op jit(solution)/shard_map/ppermute | solution.py:14
  142.2 1.3 collective-permute-start.30
  143.5 1.3 collective-permute-start.18
  144.8 4.8 %collective-permute-start.19 = (f32[4,1,256]{2,0,1:T(4,128)S(1)}, f32[4,1,256]{2,0,1:T(4,128)S(1)}, u32[]{:S(2)}, u32[]{:S(2)}) collective-permute-start(f32[4,1,256]{2,0,1:T(4,128)S(1)} %get-tuple-element.142), channel_id=1, source_target_pairs={{0,4},{4,8},{8,12},{1,5},{5,9},{9,13},{2,6},{6,10},{10,14},{3,7},{... | collective-permute-start | bytes 12296 | tf_op jit(solution)/shard_map/ppermute | solution.py:14
  149.8 1.3 collective-permute-start.32
  151.1 4.6 %collective-permute-start.33 = (f32[4,1,128]{2,1,0:T(1,128)S(1)}, f32[4,1,128]{2,1,0:T(1,128)S(1)}, u32[]{:S(2)}, u32[]{:S(2)}) collective-permute-start(f32[4,1,128]{2,1,0:T(1,128)S(1)} %get-tuple-element.158), channel_id=1, source_target_pairs={{0,4},{4,8},{8,12},{1,5},{5,9},{9,13},{2,6},{6,10},{10,14},{3,7},{... | collective-permute-start | bytes 6152 | tf_op jit(solution)/shard_map/ppermute | solution.py:14
  155.8 0.8 gather_fusion.1
  156.5 15.5 %fusion = f32[4,128,128]{2,0,1:T(4,128)S(1)} fusion(f32[128,128,128]{2,1,0:T(8,128)} %param.30, f32[128,4,128]{2,1,0:T(4,128)S(1)} %gather_fusion.1, f32[128,128]{1,0:T(8,128)S(1)} %broadcast_multiply_fusion, pred[128]{0:T(512)(128)(4,1)S(1)} %compare_and_fusion), kind=kOutput, calls=%fused_computation.3 | convolution fusion | flops 100794368 | bytes 8978560 | tf_op jit(solution)/shard_map/bij,pbj->pbi/dot_general | solution.py:92
  172.0 9.4 %fusion.93 = f32[128,4,128]{2,1,0:T(4,128)S(1)} fusion(f32[4,128,128]{2,0,1:T(4,128)S(1)} %fusion, f32[128,128,128]{2,1,0:T(8,128)} %param.30), kind=kOutput, calls=%fused_computation.210 | convolution fusion | flops 100663296 | bytes 8912896 | tf_op jit(solution)/shard_map/bij,pbi->pbj/dot_general | solution.py:100
  181.9 3.9 %collective-permute-start.28 = (f32[4,384]{1,0:T(4,128)S(1)}, f32[4,384]{1,0:T(4,128)S(1)}, u32[]{:S(2)}, u32[]{:S(2)}) collective-permute-start(f32[4,384]{1,0:T(4,128)S(1)} %pad_maximum_fusion.76), channel_id=1, source_target_pairs={{0,4},{4,8},{8,12},{1,5},{5,9},{9,13},{2,6},{6,10},{10,14},{3,7},{... | collective-permute-start | bytes 18440 | tf_op jit(solution)/shard_map/ppermute | solution.py:25
  185.8 4.6 %collective-permute-start.21 = (f32[4,34,1]{2,0,1:T(4,128)S(1)}, f32[4,34,1]{2,0,1:T(4,128)S(1)}, u32[]{:S(2)}, u32[]{:S(2)}) collective-permute-start(f32[4,34,1]{2,0,1:T(4,128)S(1)} %get-tuple-element.131), channel_id=1, source_target_pairs={{0,2},{1,3},{4,6},{5,7},{8,10},{9,11},{12,14},{13,15},{16,18},{17,... | collective-permute-start | bytes 1640 | tf_op jit(solution)/shard_map/ppermute | solution.py:14
  190.4 1.3 collective-permute-start.20
  191.7 0.6 collective-permute-done.21
  192.3 4.3 %collective-permute-done.20 = f32[4,34,1]{2,0,1:T(4,128)S(1)} collective-permute-done((f32[4,34,1]{2,0,1:T(4,128)S(1)}, f32[4,34,1]{2,0,1:T(4,128)S(1)}, u32[]{:S(2)}, u32[]{:S(2)}) %collective-permute-start.20) | collective-permute-done | bytes 576 | tf_op jit(solution)/shard_map/ppermute | solution.py:17
  196.8 1.3 collective-permute-start.22
  198.1 4.5 %collective-permute-start.23 = (f32[4,1,256]{2,0,1:T(4,128)S(1)}, f32[4,1,256]{2,0,1:T(4,128)S(1)}, u32[]{:S(2)}, u32[]{:S(2)}) collective-permute-start(f32[4,1,256]{2,0,1:T(4,128)S(1)} %get-tuple-element.140), channel_id=1, source_target_pairs={{0,4},{4,8},{8,12},{1,5},{5,9},{9,13},{2,6},{6,10},{10,14},{3,7},{... | collective-permute-start | bytes 12296 | tf_op jit(solution)/shard_map/ppermute | solution.py:14
  202.8 1.6 collective-permute-start.35
  204.3 1.3 collective-permute-start.34
  205.8 4.5 %collective-permute-start.25 = (f32[4,34,1]{2,0,1:T(4,128)S(1)}, f32[4,34,1]{2,0,1:T(4,128)S(1)}, u32[]{:S(2)}, u32[]{:S(2)}) collective-permute-start(f32[4,34,1]{2,0,1:T(4,128)S(1)} %get-tuple-element.129), channel_id=1, source_target_pairs={{0,2},{1,3},{4,6},{5,7},{8,10},{9,11},{12,14},{13,15},{16,18},{17,... | collective-permute-start | bytes 1640 | tf_op jit(solution)/shard_map/ppermute | solution.py:14
  210.4 1.3 collective-permute-start.24
  211.7 1.3 collective-permute-start.29
  213.0 4.2 %collective-permute-done.29 = f32[4,384]{1,0:T(4,128)S(1)} collective-permute-done((f32[4,384]{1,0:T(4,128)S(1)}, f32[4,384]{1,0:T(4,128)S(1)}, u32[]{:S(2)}, u32[]{:S(2)}) %collective-permute-start.29) | collective-permute-done | bytes 6176 | tf_op jit(solution)/shard_map/ppermute | solution.py:25
  217.9 19.8 %psum.31 = f32[4]{0:T(128)S(1)} all-reduce(f32[4]{0:T(128)S(1)} %add.235), channel_id=1, replica_groups=mesh['grp'=2,'ew'=4,'ns'=2,'lvl'=2] {'ew','ns'}, use_global_device_ids=true, to_apply=%region_11.13 | all-reduce | flops 4 | bytes 32 | tf_op jit(solution)/shard_map/psum | solution.py:124
  237.8 0.7 copy.51
  238.5 0.7 multiply_subtract_fusion.2
  239.2 0.7 copy.52
  (122 shorter events, 4.8 us)
Async XLA Ops:
  1.4 18.1 %collective-permute-start.9 = (f32[4,1,128]{2,1,0:T(1,128)S(1)}, f32[4,1,128]{2,1,0:T(1,128)S(1)}, u32[]{:S(2)}, u32[]{:S(2)}) collective-permute-start(f32[4,1,128]{2,1,0:T(1,128)S(1)} %get-tuple-element.165), channel_id=1, source_target_pairs={{4,0},{8,4},{12,8},{5,1},{9,5},{13,9},{6,2},{10,6},{14,10},{7,3},{... | collective-permute-start | bytes 6152 | tf_op jit(solution)/shard_map/ppermute | solution.py:17
  2.7 16.8 %collective-permute-start.8 = (f32[4,1,128]{2,1,0:T(1,128)S(1)}, f32[4,1,128]{2,1,0:T(1,128)S(1)}, u32[]{:S(2)}, u32[]{:S(2)}) collective-permute-start(f32[4,1,128]{2,1,0:T(1,128)S(1)} %get-tuple-element.164), channel_id=1, source_target_pairs={{0,4},{4,8},{8,12},{1,5},{5,9},{9,13},{2,6},{6,10},{10,14},{3,7},{... | collective-permute-start | bytes 6152 | tf_op jit(solution)/shard_map/ppermute | solution.py:14
  9.3 26.1 %collective-permute-start = (f32[4,1,256]{2,0,1:T(4,128)S(1)}, f32[4,1,256]{2,0,1:T(4,128)S(1)}, u32[]{:S(2)}, u32[]{:S(2)}) collective-permute-start(f32[4,1,256]{2,0,1:T(4,128)S(1)} %get-tuple-element.147), channel_id=1, source_target_pairs={{4,0},{8,4},{12,8},{5,1},{9,5},{13,9},{6,2},{10,6},{14,10},{7,3},{... | collective-permute-start | bytes 12296 | tf_op jit(solution)/shard_map/ppermute | solution.py:17
  10.6 24.8 %collective-permute-start.1 = (f32[4,1,256]{2,0,1:T(4,128)S(1)}, f32[4,1,256]{2,0,1:T(4,128)S(1)}, u32[]{:S(2)}, u32[]{:S(2)}) collective-permute-start(f32[4,1,256]{2,0,1:T(4,128)S(1)} %get-tuple-element.146), channel_id=1, source_target_pairs={{0,4},{4,8},{8,12},{1,5},{5,9},{9,13},{2,6},{6,10},{10,14},{3,7},{... | collective-permute-start | bytes 12296 | tf_op jit(solution)/shard_map/ppermute | solution.py:14
  19.6 5.6 %collective-permute-start.13 = (f32[4,18,1]{2,1,0:T(8,128)S(1)}, f32[4,18,1]{2,1,0:T(8,128)S(1)}, u32[]{:S(2)}, u32[]{:S(2)}) collective-permute-start(f32[4,18,1]{2,1,0:T(8,128)S(1)} %get-tuple-element.155), channel_id=1, source_target_pairs={{0,2},{1,3},{4,6},{5,7},{8,10},{9,11},{12,14},{13,15},{16,18},{17,... | collective-permute-start | bytes 872 | tf_op jit(solution)/shard_map/ppermute | solution.py:14
  23.5 6.0 %collective-permute-start.12 = (f32[4,18,1]{2,1,0:T(8,128)S(1)}, f32[4,18,1]{2,1,0:T(8,128)S(1)}, u32[]{:S(2)}, u32[]{:S(2)}) collective-permute-start(f32[4,18,1]{2,1,0:T(8,128)S(1)} %get-tuple-element.154), channel_id=1, source_target_pairs={{2,0},{3,1},{6,4},{7,5},{10,8},{11,9},{14,12},{15,13},{18,16},{19,... | collective-permute-start | bytes 872 | tf_op jit(solution)/shard_map/ppermute | solution.py:17
  29.6 37.6 %collective-permute-start.14 = (f32[4,1,128]{2,1,0:T(1,128)S(1)}, f32[4,1,128]{2,1,0:T(1,128)S(1)}, u32[]{:S(2)}, u32[]{:S(2)}) collective-permute-start(f32[4,1,128]{2,1,0:T(1,128)S(1)} %get-tuple-element.163), channel_id=1, source_target_pairs={{4,0},{8,4},{12,8},{5,1},{9,5},{13,9},{6,2},{10,6},{14,10},{7,3},{... | collective-permute-start | bytes 6152 | tf_op jit(solution)/shard_map/ppermute | solution.py:17
  30.9 36.4 %collective-permute-start.15 = (f32[4,1,128]{2,1,0:T(1,128)S(1)}, f32[4,1,128]{2,1,0:T(1,128)S(1)}, u32[]{:S(2)}, u32[]{:S(2)}) collective-permute-start(f32[4,1,128]{2,1,0:T(1,128)S(1)} %get-tuple-element.162), channel_id=1, source_target_pairs={{0,4},{4,8},{8,12},{1,5},{5,9},{9,13},{2,6},{6,10},{10,14},{3,7},{... | collective-permute-start | bytes 6152 | tf_op jit(solution)/shard_map/ppermute | solution.py:14
  36.3 16.4 %copy-start = (f32[128,128,128]{2,1,0:T(8,128)S(1)}, f32[128,128,128]{2,1,0:T(8,128)}, u32[]{:S(2)}) copy-start(f32[128,128,128]{2,1,0:T(8,128)} %param.30) | copy-start | bytes 25165828
  36.3 23.7 %copy-start.3 = (s32[128]{0:T(128)S(1)}, s32[128]{0:T(128)}, u32[]{:S(2)}) copy-start(s32[128]{0:T(128)} %param.32) | copy-start | bytes 1540
  36.3 56.5 %copy-start.1 = (s32[4,32,256]{2,1,0:T(8,128)S(1)}, s32[4,32,256]{2,1,0:T(8,128)}, u32[]{:S(2)}) copy-start(s32[4,32,256]{2,1,0:T(8,128)} %param.26) | copy-start | bytes 393220
  52.7 40.5 %copy-start.2 = (s32[4,16,128]{2,1,0:T(8,128)S(1)}, s32[4,16,128]{2,1,0:T(8,128)}, u32[]{:S(2)}) copy-start(s32[4,16,128]{2,1,0:T(8,128)} %param.27) | copy-start | bytes 98308
  60.6 26.6 %collective-permute-start.10 = (f32[4,384]{1,0:T(4,128)S(1)}, f32[4,384]{1,0:T(4,128)S(1)}, u32[]{:S(2)}, u32[]{:S(2)}) collective-permute-start(f32[4,384]{1,0:T(4,128)S(1)} %pad_maximum_fusion.74), channel_id=1, source_target_pairs={{0,4},{4,8},{8,12},{1,5},{5,9},{9,13},{2,6},{6,10},{10,14},{3,7},{... | collective-permute-start | bytes 18440 | tf_op jit(solution)/shard_map/ppermute | solution.py:25
  64.1 3.5 %collective-permute-start.3 = (f32[4,34,1]{2,0,1:T(4,128)S(1)}, f32[4,34,1]{2,0,1:T(4,128)S(1)}, u32[]{:S(2)}, u32[]{:S(2)}) collective-permute-start(f32[4,34,1]{2,0,1:T(4,128)S(1)} %get-tuple-element.137), channel_id=1, source_target_pairs={{0,2},{1,3},{4,6},{5,7},{8,10},{9,11},{12,14},{13,15},{16,18},{17,... | collective-permute-start | bytes 1640 | tf_op jit(solution)/shard_map/ppermute | solution.py:14
  65.7 6.4 %collective-permute-start.2 = (f32[4,34,1]{2,0,1:T(4,128)S(1)}, f32[4,34,1]{2,0,1:T(4,128)S(1)}, u32[]{:S(2)}, u32[]{:S(2)}) collective-permute-start(f32[4,34,1]{2,0,1:T(4,128)S(1)} %get-tuple-element.136), channel_id=1, source_target_pairs={{2,0},{3,1},{6,4},{7,5},{10,8},{11,9},{14,12},{15,13},{18,16},{19,... | collective-permute-start | bytes 1640 | tf_op jit(solution)/shard_map/ppermute | solution.py:17
  72.4 8.8 %collective-permute-start.4 = (f32[4,1,256]{2,0,1:T(4,128)S(1)}, f32[4,1,256]{2,0,1:T(4,128)S(1)}, u32[]{:S(2)}, u32[]{:S(2)}) collective-permute-start(f32[4,1,256]{2,0,1:T(4,128)S(1)} %get-tuple-element.145), channel_id=1, source_target_pairs={{4,0},{8,4},{12,8},{5,1},{9,5},{13,9},{6,2},{10,6},{14,10},{7,3},{... | collective-permute-start | bytes 12296 | tf_op jit(solution)/shard_map/ppermute | solution.py:17
  73.7 7.5 %collective-permute-start.5 = (f32[4,1,256]{2,0,1:T(4,128)S(1)}, f32[4,1,256]{2,0,1:T(4,128)S(1)}, u32[]{:S(2)}, u32[]{:S(2)}) collective-permute-start(f32[4,1,256]{2,0,1:T(4,128)S(1)} %get-tuple-element.144), channel_id=1, source_target_pairs={{0,4},{4,8},{8,12},{1,5},{5,9},{9,13},{2,6},{6,10},{10,14},{3,7},{... | collective-permute-start | bytes 12296 | tf_op jit(solution)/shard_map/ppermute | solution.py:14
  78.3 14.9 %collective-permute-start.17 = (f32[4,18,1]{2,1,0:T(8,128)S(1)}, f32[4,18,1]{2,1,0:T(8,128)S(1)}, u32[]{:S(2)}, u32[]{:S(2)}) collective-permute-start(f32[4,18,1]{2,1,0:T(8,128)S(1)} %get-tuple-element.153), channel_id=1, source_target_pairs={{0,2},{1,3},{4,6},{5,7},{8,10},{9,11},{12,14},{13,15},{16,18},{17,... | collective-permute-start | bytes 872 | tf_op jit(solution)/shard_map/ppermute | solution.py:14
  79.9 13.4 %collective-permute-start.16 = (f32[4,18,1]{2,1,0:T(8,128)S(1)}, f32[4,18,1]{2,1,0:T(8,128)S(1)}, u32[]{:S(2)}, u32[]{:S(2)}) collective-permute-start(f32[4,18,1]{2,1,0:T(8,128)S(1)} %get-tuple-element.152), channel_id=1, source_target_pairs={{2,0},{3,1},{6,4},{7,5},{10,8},{11,9},{14,12},{15,13},{18,16},{19,... | collective-permute-start | bytes 872 | tf_op jit(solution)/shard_map/ppermute | solution.py:17
  81.3 11.4 %collective-permute-start.7 = (f32[4,34,1]{2,0,1:T(4,128)S(1)}, f32[4,34,1]{2,0,1:T(4,128)S(1)}, u32[]{:S(2)}, u32[]{:S(2)}) collective-permute-start(f32[4,34,1]{2,0,1:T(4,128)S(1)} %get-tuple-element.135), channel_id=1, source_target_pairs={{0,2},{1,3},{4,6},{5,7},{8,10},{9,11},{12,14},{13,15},{16,18},{17,... | collective-permute-start | bytes 1640 | tf_op jit(solution)/shard_map/ppermute | solution.py:14
  85.9 6.9 %collective-permute-start.6 = (f32[4,34,1]{2,0,1:T(4,128)S(1)}, f32[4,34,1]{2,0,1:T(4,128)S(1)}, u32[]{:S(2)}, u32[]{:S(2)}) collective-permute-start(f32[4,34,1]{2,0,1:T(4,128)S(1)} %get-tuple-element.134), channel_id=1, source_target_pairs={{2,0},{3,1},{6,4},{7,5},{10,8},{11,9},{14,12},{15,13},{18,16},{19,... | collective-permute-start | bytes 1640 | tf_op jit(solution)/shard_map/ppermute | solution.py:17
  87.2 5.5 %collective-permute-start.11 = (f32[4,384]{1,0:T(4,128)S(1)}, f32[4,384]{1,0:T(4,128)S(1)}, u32[]{:S(2)}, u32[]{:S(2)}) collective-permute-start(f32[4,384]{1,0:T(4,128)S(1)} %pad_maximum_fusion.75), channel_id=1, source_target_pairs={{4,0},{8,4},{12,8},{5,1},{9,5},{13,9},{6,2},{10,6},{14,10},{7,3},{... | collective-permute-start | bytes 18440 | tf_op jit(solution)/shard_map/ppermute | solution.py:25
  131.3 5.9 %collective-permute-start.27 = (f32[4,1,128]{2,1,0:T(1,128)S(1)}, f32[4,1,128]{2,1,0:T(1,128)S(1)}, u32[]{:S(2)}, u32[]{:S(2)}) collective-permute-start(f32[4,1,128]{2,1,0:T(1,128)S(1)} %get-tuple-element.161), channel_id=1, source_target_pairs={{4,0},{8,4},{12,8},{5,1},{9,5},{13,9},{6,2},{10,6},{14,10},{7,3},{... | collective-permute-start | bytes 6152 | tf_op jit(solution)/shard_map/ppermute | solution.py:17
  132.6 5.8 %collective-permute-start.26 = (f32[4,1,128]{2,1,0:T(1,128)S(1)}, f32[4,1,128]{2,1,0:T(1,128)S(1)}, u32[]{:S(2)}, u32[]{:S(2)}) collective-permute-start(f32[4,1,128]{2,1,0:T(1,128)S(1)} %get-tuple-element.160), channel_id=1, source_target_pairs={{0,4},{4,8},{8,12},{1,5},{5,9},{9,13},{2,6},{6,10},{10,14},{3,7},{... | collective-permute-start | bytes 6152 | tf_op jit(solution)/shard_map/ppermute | solution.py:14
  138.5 11.1 %collective-permute-start.31 = (f32[4,18,1]{2,1,0:T(8,128)S(1)}, f32[4,18,1]{2,1,0:T(8,128)S(1)}, u32[]{:S(2)}, u32[]{:S(2)}) collective-permute-start(f32[4,18,1]{2,1,0:T(8,128)S(1)} %get-tuple-element.151), channel_id=1, source_target_pairs={{0,2},{1,3},{4,6},{5,7},{8,10},{9,11},{12,14},{13,15},{16,18},{17,... | collective-permute-start | bytes 872 | tf_op jit(solution)/shard_map/ppermute | solution.py:14
  142.2 7.4 %collective-permute-start.30 = (f32[4,18,1]{2,1,0:T(8,128)S(1)}, f32[4,18,1]{2,1,0:T(8,128)S(1)}, u32[]{:S(2)}, u32[]{:S(2)}) collective-permute-start(f32[4,18,1]{2,1,0:T(8,128)S(1)} %get-tuple-element.150), channel_id=1, source_target_pairs={{2,0},{3,1},{6,4},{7,5},{10,8},{11,9},{14,12},{15,13},{18,16},{19,... | collective-permute-start | bytes 872 | tf_op jit(solution)/shard_map/ppermute | solution.py:17
  143.5 12.1 %collective-permute-start.18 = (f32[4,1,256]{2,0,1:T(4,128)S(1)}, f32[4,1,256]{2,0,1:T(4,128)S(1)}, u32[]{:S(2)}, u32[]{:S(2)}) collective-permute-start(f32[4,1,256]{2,0,1:T(4,128)S(1)} %get-tuple-element.143), channel_id=1, source_target_pairs={{4,0},{8,4},{12,8},{5,1},{9,5},{13,9},{6,2},{10,6},{14,10},{7,3},{... | collective-permute-start | bytes 12296 | tf_op jit(solution)/shard_map/ppermute | solution.py:17
  144.8 10.8 %collective-permute-start.19 = (f32[4,1,256]{2,0,1:T(4,128)S(1)}, f32[4,1,256]{2,0,1:T(4,128)S(1)}, u32[]{:S(2)}, u32[]{:S(2)}) collective-permute-start(f32[4,1,256]{2,0,1:T(4,128)S(1)} %get-tuple-element.142), channel_id=1, source_target_pairs={{0,4},{4,8},{8,12},{1,5},{5,9},{9,13},{2,6},{6,10},{10,14},{3,7},{... | collective-permute-start | bytes 12296 | tf_op jit(solution)/shard_map/ppermute | solution.py:14
  149.8 41.9 %collective-permute-start.32 = (f32[4,1,128]{2,1,0:T(1,128)S(1)}, f32[4,1,128]{2,1,0:T(1,128)S(1)}, u32[]{:S(2)}, u32[]{:S(2)}) collective-permute-start(f32[4,1,128]{2,1,0:T(1,128)S(1)} %get-tuple-element.159), channel_id=1, source_target_pairs={{4,0},{8,4},{12,8},{5,1},{9,5},{13,9},{6,2},{10,6},{14,10},{7,3},{... | collective-permute-start | bytes 6152 | tf_op jit(solution)/shard_map/ppermute | solution.py:17
  151.1 40.6 %collective-permute-start.33 = (f32[4,1,128]{2,1,0:T(1,128)S(1)}, f32[4,1,128]{2,1,0:T(1,128)S(1)}, u32[]{:S(2)}, u32[]{:S(2)}) collective-permute-start(f32[4,1,128]{2,1,0:T(1,128)S(1)} %get-tuple-element.158), channel_id=1, source_target_pairs={{0,4},{4,8},{8,12},{1,5},{5,9},{9,13},{2,6},{6,10},{10,14},{3,7},{... | collective-permute-start | bytes 6152 | tf_op jit(solution)/shard_map/ppermute | solution.py:14
  181.9 29.8 %collective-permute-start.28 = (f32[4,384]{1,0:T(4,128)S(1)}, f32[4,384]{1,0:T(4,128)S(1)}, u32[]{:S(2)}, u32[]{:S(2)}) collective-permute-start(f32[4,384]{1,0:T(4,128)S(1)} %pad_maximum_fusion.76), channel_id=1, source_target_pairs={{0,4},{4,8},{8,12},{1,5},{5,9},{9,13},{2,6},{6,10},{10,14},{3,7},{... | collective-permute-start | bytes 18440 | tf_op jit(solution)/shard_map/ppermute | solution.py:25
  185.8 6.5 %collective-permute-start.21 = (f32[4,34,1]{2,0,1:T(4,128)S(1)}, f32[4,34,1]{2,0,1:T(4,128)S(1)}, u32[]{:S(2)}, u32[]{:S(2)}) collective-permute-start(f32[4,34,1]{2,0,1:T(4,128)S(1)} %get-tuple-element.131), channel_id=1, source_target_pairs={{0,2},{1,3},{4,6},{5,7},{8,10},{9,11},{12,14},{13,15},{16,18},{17,... | collective-permute-start | bytes 1640 | tf_op jit(solution)/shard_map/ppermute | solution.py:14
  190.4 6.2 %collective-permute-start.20 = (f32[4,34,1]{2,0,1:T(4,128)S(1)}, f32[4,34,1]{2,0,1:T(4,128)S(1)}, u32[]{:S(2)}, u32[]{:S(2)}) collective-permute-start(f32[4,34,1]{2,0,1:T(4,128)S(1)} %get-tuple-element.130), channel_id=1, source_target_pairs={{2,0},{3,1},{6,4},{7,5},{10,8},{11,9},{14,12},{15,13},{18,16},{19,... | collective-permute-start | bytes 1640 | tf_op jit(solution)/shard_map/ppermute | solution.py:17
  196.8 8.8 %collective-permute-start.22 = (f32[4,1,256]{2,0,1:T(4,128)S(1)}, f32[4,1,256]{2,0,1:T(4,128)S(1)}, u32[]{:S(2)}, u32[]{:S(2)}) collective-permute-start(f32[4,1,256]{2,0,1:T(4,128)S(1)} %get-tuple-element.141), channel_id=1, source_target_pairs={{4,0},{8,4},{12,8},{5,1},{9,5},{13,9},{6,2},{10,6},{14,10},{7,3},{... | collective-permute-start | bytes 12296 | tf_op jit(solution)/shard_map/ppermute | solution.py:17
  198.1 7.5 %collective-permute-start.23 = (f32[4,1,256]{2,0,1:T(4,128)S(1)}, f32[4,1,256]{2,0,1:T(4,128)S(1)}, u32[]{:S(2)}, u32[]{:S(2)}) collective-permute-start(f32[4,1,256]{2,0,1:T(4,128)S(1)} %get-tuple-element.140), channel_id=1, source_target_pairs={{0,4},{4,8},{8,12},{1,5},{5,9},{9,13},{2,6},{6,10},{10,14},{3,7},{... | collective-permute-start | bytes 12296 | tf_op jit(solution)/shard_map/ppermute | solution.py:14
  202.8 14.9 %collective-permute-start.35 = (f32[4,18,1]{2,1,0:T(8,128)S(1)}, f32[4,18,1]{2,1,0:T(8,128)S(1)}, u32[]{:S(2)}, u32[]{:S(2)}) collective-permute-start(f32[4,18,1]{2,1,0:T(8,128)S(1)} %get-tuple-element.149), channel_id=1, source_target_pairs={{0,2},{1,3},{4,6},{5,7},{8,10},{9,11},{12,14},{13,15},{16,18},{17,... | collective-permute-start | bytes 872 | tf_op jit(solution)/shard_map/ppermute | solution.py:14
  204.3 13.3 %collective-permute-start.34 = (f32[4,18,1]{2,1,0:T(8,128)S(1)}, f32[4,18,1]{2,1,0:T(8,128)S(1)}, u32[]{:S(2)}, u32[]{:S(2)}) collective-permute-start(f32[4,18,1]{2,1,0:T(8,128)S(1)} %get-tuple-element.148), channel_id=1, source_target_pairs={{2,0},{3,1},{6,4},{7,5},{10,8},{11,9},{14,12},{15,13},{18,16},{19,... | collective-permute-start | bytes 872 | tf_op jit(solution)/shard_map/ppermute | solution.py:17
  205.8 11.4 %collective-permute-start.25 = (f32[4,34,1]{2,0,1:T(4,128)S(1)}, f32[4,34,1]{2,0,1:T(4,128)S(1)}, u32[]{:S(2)}, u32[]{:S(2)}) collective-permute-start(f32[4,34,1]{2,0,1:T(4,128)S(1)} %get-tuple-element.129), channel_id=1, source_target_pairs={{0,2},{1,3},{4,6},{5,7},{8,10},{9,11},{12,14},{13,15},{16,18},{17,... | collective-permute-start | bytes 1640 | tf_op jit(solution)/shard_map/ppermute | solution.py:14
  210.4 6.9 %collective-permute-start.24 = (f32[4,34,1]{2,0,1:T(4,128)S(1)}, f32[4,34,1]{2,0,1:T(4,128)S(1)}, u32[]{:S(2)}, u32[]{:S(2)}) collective-permute-start(f32[4,34,1]{2,0,1:T(4,128)S(1)} %get-tuple-element.128), channel_id=1, source_target_pairs={{2,0},{3,1},{6,4},{7,5},{10,8},{11,9},{14,12},{15,13},{18,16},{19,... | collective-permute-start | bytes 1640 | tf_op jit(solution)/shard_map/ppermute | solution.py:17
  211.7 5.5 %collective-permute-start.29 = (f32[4,384]{1,0:T(4,128)S(1)}, f32[4,384]{1,0:T(4,128)S(1)}, u32[]{:S(2)}, u32[]{:S(2)}) collective-permute-start(f32[4,384]{1,0:T(4,128)S(1)} %pad_maximum_fusion.77), channel_id=1, source_target_pairs={{4,0},{8,4},{12,8},{5,1},{9,5},{13,9},{6,2},{10,6},{14,10},{7,3},{... | collective-permute-start | bytes 18440 | tf_op jit(solution)/shard_map/ppermute | solution.py:25
where the time goes:
time: 241 us; the launch traced here: 240 us
  starting transfers between devices  94.4 us (39%)
  blocking collectives  56.9 us (24%)
  matrix products  49 us (20%)
  waiting for transfers between devices  24 us (10%)
  other arithmetic  9.25 us (4%)
  local copies, waits for them, and re-layouts  4.04 us (2%)
    ppermute x16, starting transfers between devices, with_halo(): lax.ppermute(lax.slice_in_dim(block, block.shape[dim] - width, None, axis...  63.6 us
    psum x2, blocking collectives, squares(): lax.psum(local_products(first_fine, first_coarse, first_fine, first_coars...  37.1 us
    dot_general x2, matrix products, local(): jnp.einsum('bij,pbj->pbi', phi_tiles, picked, precision=lax.Precision.HIG...  31.8 us
    ppermute x16, starting transfers between devices, with_halo(): lax.ppermute(lax.slice_in_dim(block, 0, width, axis=dim), axis, backward)  20.9 us
    psum x1, blocking collectives, local(): lax.psum(local_products(direction_fine, direction_coarse, image_fine, ima...  19.8 us
    dot_general x2, matrix products, local(): jnp.einsum('bij,pbi->pbj', phi_tiles, scaled, precision=lax.Precision.HIG...  16.7 us
    ppermute x16, waiting for transfers between devices, with_halo(): lax.ppermute(lax.slice_in_dim(block, 0, width, axis=dim), axis, backward)  13 us
    ppermute x4, starting transfers between devices, shifted(): return lax.ppermute(block, axis, route)  9.99 us
  transfers between devices with their start and end apart: 36, of which 9 were waited for; matrix products, arithmetic and copies ran while one was open for 24% of the time, Pallas kernels for 0%

commit v1 on v0

--- a/solution.py
+++ b/solution.py
@@ -122,7 +122,10 @@
         image_fine = prior_fine + inner_fine
         image_coarse = prior_coarse + inner_coarse
         curve = lax.psum(
-            local_products(direction_fine, direction_coarse, image_fine, image_coarse), ("ew", "ns")
+            lax.psum(
+                local_products(direction_fine, direction_coarse, image_fine, image_coarse), "ns"
+            ),
+            "ew",
         )
         alpha = (norm_now / curve)[:, None, None]
         solve_fine = solve_fine + alpha * direction_fine

time: 241 us -> 249 us (1.033)
  blocking collectives: 56.9 us -> 65.5 us
    psum x0 -> x2, blocking collectives: none -> 16.7 us  [local(): lax.psum(lax.psum(local_products(direction_fine, direction_coarse, image_...]
    psum x1 -> x2, blocking collectives: 19.8 us -> 11.1 us  [local(): lax.psum(local_products(direction_fine, direction_coarse, image_fine, ima...]
  transfers between devices with their start and end apart: 36 -> 36, of which waited for: 9 -> 9; matrix products, arithmetic and copies ran while one was open for 24% -> 23% of each run, Pallas kernels for 0% -> 0%
where the time goes in v1:
time: 249 us; the launch traced here: 247 us
  starting transfers between devices  93.2 us (37%)
  blocking collectives  65.5 us (26%)
  matrix products  49 us (20%)
  waiting for transfers between devices  24 us (10%)
  other arithmetic  9.25 us (4%)
  local copies, waits for them, and re-layouts  4.04 us (2%)
    ppermute x16, starting transfers between devices, with_halo(): lax.ppermute(lax.slice_in_dim(block, block.shape[dim] - width, None, axis...  62.3 us
    psum x2, blocking collectives, squares(): lax.psum(local_products(first_fine, first_coarse, first_fine, first_coars...  37.7 us
    dot_general x2, matrix products, local(): jnp.einsum('bij,pbj->pbi', phi_tiles, picked, precision=lax.Precision.HIG...  31.8 us
    ppermute x16, starting transfers between devices, with_halo(): lax.ppermute(lax.slice_in_dim(block, 0, width, axis=dim), axis, backward)  20.9 us
    psum x2, blocking collectives, local(): lax.psum(lax.psum(local_products(direction_fine, direction_coarse, image_...  16.7 us
    dot_general x2, matrix products, local(): jnp.einsum('bij,pbi->pbj', phi_tiles, scaled, precision=lax.Precision.HIG...  16.7 us
    ppermute x16, waiting for transfers between devices, with_halo(): lax.ppermute(lax.slice_in_dim(block, 0, width, axis=dim), axis, backward)  13 us
    psum x2, blocking collectives, local(): lax.psum(local_products(direction_fine, direction_coarse, image_fine, ima...  11.1 us
  transfers between devices with their start and end apart: 36, of which 9 were waited for; matrix products, arithmetic and copies ran while one was open for 23% of the time, Pallas kernels for 0%

profile of v1, /device:TPU:0, one launch (start us, length us, event | category | flops | bytes accessed | tf_op | source)
XLA Modules:
  0.0 247.3 jit_solution(13502533659622694613)
XLA Ops:
  0.6 0.8 add_convert_fusion
  1.4 1.3 collective-permute-start.9
  2.7 5.6 %collective-permute-start.8 = (f32[4,1,128]{2,1,0:T(1,128)S(1)}, f32[4,1,128]{2,1,0:T(1,128)S(1)}, u32[]{:S(2)}, u32[]{:S(2)}) collective-permute-start(f32[4,1,128]{2,1,0:T(1,128)S(1)} %get-tuple-element.162), channel_id=1, source_target_pairs={{0,4},{4,8},{8,12},{1,5},{5,9},{9,13},{2,6},{6,10},{10,14},{3,7},{... | collective-permute-start | bytes 6152 | tf_op jit(solution)/shard_map/ppermute | solution.py:14
  8.3 1.0 fusion.30
  9.3 1.3 collective-permute-start
  10.6 4.6 %collective-permute-start.1 = (f32[4,1,256]{2,0,1:T(4,128)S(1)}, f32[4,1,256]{2,0,1:T(4,128)S(1)}, u32[]{:S(2)}, u32[]{:S(2)}) collective-permute-start(f32[4,1,256]{2,0,1:T(4,128)S(1)} %get-tuple-element.144), channel_id=1, source_target_pairs={{0,4},{4,8},{8,12},{1,5},{5,9},{9,13},{2,6},{6,10},{10,14},{3,7},{... | collective-permute-start | bytes 12296 | tf_op jit(solution)/shard_map/ppermute | solution.py:14
  15.2 0.7 compare_select_fusion
  16.5 0.8 broadcast_add_fusion
  17.2 0.7 broadcast_add_fusion.1
  17.9 0.9 broadcast_multiply_fusion
  18.9 0.7 compare_and_fusion
  19.6 3.8 %collective-permute-start.13 = (f32[4,18,1]{2,1,0:T(8,128)S(1)}, f32[4,18,1]{2,1,0:T(8,128)S(1)}, u32[]{:S(2)}, u32[]{:S(2)}) collective-permute-start(f32[4,18,1]{2,1,0:T(8,128)S(1)} %get-tuple-element.153), channel_id=1, source_target_pairs={{0,2},{1,3},{4,6},{5,7},{8,10},{9,11},{12,14},{13,15},{16,18},{17,... | collective-permute-start | bytes 872 | tf_op jit(solution)/shard_map/ppermute | solution.py:14
  23.5 1.3 collective-permute-start.12
  25.2 4.3 %collective-permute-done.12 = f32[4,18,1]{2,1,0:T(8,128)S(1)} collective-permute-done((f32[4,18,1]{2,1,0:T(8,128)S(1)}, f32[4,18,1]{2,1,0:T(8,128)S(1)}, u32[]{:S(2)}, u32[]{:S(2)}) %collective-permute-start.12) | collective-permute-done | bytes 320 | tf_op jit(solution)/shard_map/ppermute | solution.py:17
  29.6 1.3 collective-permute-start.14
  30.9 4.5 %collective-permute-start.15 = (f32[4,1,128]{2,1,0:T(1,128)S(1)}, f32[4,1,128]{2,1,0:T(1,128)S(1)}, u32[]{:S(2)}, u32[]{:S(2)}) collective-permute-start(f32[4,1,128]{2,1,0:T(1,128)S(1)} %get-tuple-element.160), channel_id=1, source_target_pairs={{0,4},{4,8},{8,12},{1,5},{5,9},{9,13},{2,6},{6,10},{10,14},{3,7},{... | collective-permute-start | bytes 6152 | tf_op jit(solution)/shard_map/ppermute | solution.py:14
  35.5 0.8 gather_fusion
  36.3 16.4 %fusion.1 = f32[4,128,128]{2,0,1:T(4,128)S(1)} fusion(f32[128,128,128]{2,1,0:T(8,128)} %param.30, f32[128,4,128]{2,1,0:T(4,128)S(1)} %gather_fusion, f32[128,128]{1,0:T(8,128)S(1)} %broadcast_multiply_fusion, pred[128]{0:T(512)(128)(4,1)S(1)} %compare_and_fusion), kind=kOutput, calls=%fused_computation.5 | convolution fusion | flops 100794368 | bytes 8978560 | tf_op jit(solution)/shard_map/bij,pbj->pbi/dot_general | solution.py:92
  52.7 7.3 %fusion.92 = f32[128,4,128]{2,1,0:T(4,128)S(1)} fusion(f32[4,128,128]{2,0,1:T(4,128)S(1)} %fusion.1, f32[128,128,128]{2,1,0:T(8,128)S(1)} %copy-done), kind=kOutput, calls=%fused_computation.209 | convolution fusion | flops 100663296 | bytes 8912896 | tf_op jit(solution)/shard_map/bij,pbi->pbj/dot_general | solution.py:100
  60.6 3.5 %collective-permute-start.10 = (f32[4,384]{1,0:T(4,128)S(1)}, f32[4,384]{1,0:T(4,128)S(1)}, u32[]{:S(2)}, u32[]{:S(2)}) collective-permute-start(f32[4,384]{1,0:T(4,128)S(1)} %pad_maximum_fusion.74), channel_id=1, source_target_pairs={{0,4},{4,8},{8,12},{1,5},{5,9},{9,13},{2,6},{6,10},{10,14},{3,7},{... | collective-permute-start | bytes 18440 | tf_op jit(solution)/shard_map/ppermute | solution.py:25
  64.1 1.6 collective-permute-start.3
  65.7 1.5 collective-permute-start.2
  67.7 4.5 %collective-permute-done.2 = f32[4,34,1]{2,0,1:T(4,128)S(1)} collective-permute-done((f32[4,34,1]{2,0,1:T(4,128)S(1)}, f32[4,34,1]{2,0,1:T(4,128)S(1)}, u32[]{:S(2)}, u32[]{:S(2)}) %collective-permute-start.2) | collective-permute-done | bytes 576 | tf_op jit(solution)/shard_map/ppermute | solution.py:17
  72.4 1.3 collective-permute-start.4
  73.7 4.5 %collective-permute-start.5 = (f32[4,1,256]{2,0,1:T(4,128)S(1)}, f32[4,1,256]{2,0,1:T(4,128)S(1)}, u32[]{:S(2)}, u32[]{:S(2)}) collective-permute-start(f32[4,1,256]{2,0,1:T(4,128)S(1)} %get-tuple-element.142), channel_id=1, source_target_pairs={{0,4},{4,8},{8,12},{1,5},{5,9},{9,13},{2,6},{6,10},{10,14},{3,7},{... | collective-permute-start | bytes 12296 | tf_op jit(solution)/shard_map/ppermute | solution.py:14
  78.3 1.6 collective-permute-start.17
  79.9 1.3 collective-permute-start.16
  81.3 4.5 %collective-permute-start.7 = (f32[4,34,1]{2,0,1:T(4,128)S(1)}, f32[4,34,1]{2,0,1:T(4,128)S(1)}, u32[]{:S(2)}, u32[]{:S(2)}) collective-permute-start(f32[4,34,1]{2,0,1:T(4,128)S(1)} %get-tuple-element.133), channel_id=1, source_target_pairs={{0,2},{1,3},{4,6},{5,7},{8,10},{9,11},{12,14},{13,15},{16,18},{17,... | collective-permute-start | bytes 1640 | tf_op jit(solution)/shard_map/ppermute | solution.py:14
  85.9 1.3 collective-permute-start.6
  87.2 1.3 collective-permute-start.11
  88.6 4.2 %collective-permute-done.11 = f32[4,384]{1,0:T(4,128)S(1)} collective-permute-done((f32[4,384]{1,0:T(4,128)S(1)}, f32[4,384]{1,0:T(4,128)S(1)}, u32[]{:S(2)}, u32[]{:S(2)}) %collective-permute-start.11) | collective-permute-done | bytes 6176 | tf_op jit(solution)/shard_map/ppermute | solution.py:25
  93.5 5.5 %psum.43 = f32[4]{0:T(128)S(1)} all-reduce(f32[4]{0:T(128)S(1)} %add.217), channel_id=1, replica_groups=mesh['grp'=2,'ew'=4,'ns'=2,'lvl'=2] {'ns'}, use_global_device_ids=true, to_apply=%region_5.7 | all-reduce | flops 4 | bytes 32 | tf_op jit(solution)/shard_map/psum | solution.py:125
  99.0 19.1 %psum.42 = f32[4]{0:T(128)S(1)} all-reduce(f32[4]{0:T(128)S(1)} %add.196), channel_id=1, replica_groups=mesh['grp'=2,'ew'=4,'ns'=2,'lvl'=2] {'ew','ns'}, use_global_device_ids=true, to_apply=%region_2.0 | all-reduce | flops 4 | bytes 32 | tf_op jit(solution)/shard_map/psum | solution.py:77
  118.2 8.4 %psum.44 = f32[4]{0:T(128)S(1)} all-reduce(f32[4]{0:T(128)S(1)} %psum.43), channel_id=1, replica_groups=mesh['grp'=2,'ew'=4,'ns'=2,'lvl'=2] {'ew'}, use_global_device_ids=true, to_apply=%region_6.8 | all-reduce | flops 4 | bytes 32 | tf_op jit(solution)/shard_map/psum | solution.py:124
  127.0 18.5 %psum.45 = f32[4]{0:T(128)S(1)} all-reduce(f32[4]{0:T(128)S(1)} %add.218), channel_id=1, replica_groups=mesh['grp'=2,'ew'=4,'ns'=2,'lvl'=2] {'ew','ns'}, use_global_device_ids=true, to_apply=%region_9.11 | all-reduce | flops 4 | bytes 32 | tf_op jit(solution)/shard_map/psum | solution.py:77
  145.8 1.3 collective-permute-start.27
  147.1 4.5 %collective-permute-start.26 = (f32[4,1,128]{2,1,0:T(1,128)S(1)}, f32[4,1,128]{2,1,0:T(1,128)S(1)}, u32[]{:S(2)}, u32[]{:S(2)}) collective-permute-start(f32[4,1,128]{2,1,0:T(1,128)S(1)} %get-tuple-element.158), channel_id=1, source_target_pairs={{0,4},{4,8},{8,12},{1,5},{5,9},{9,13},{2,6},{6,10},{10,14},{3,7},{... | collective-permute-start | bytes 6152 | tf_op jit(solution)/shard_map/ppermute | solution.py:14
  151.7 1.2 collective-permute-done.26
  153.0 2.5 %collective-permute-start.31 = (f32[4,18,1]{2,1,0:T(8,128)S(1)}, f32[4,18,1]{2,1,0:T(8,128)S(1)}, u32[]{:S(2)}, u32[]{:S(2)}) collective-permute-start(f32[4,18,1]{2,1,0:T(8,128)S(1)} %get-tuple-element.149), channel_id=1, source_target_pairs={{0,2},{1,3},{4,6},{5,7},{8,10},{9,11},{12,14},{13,15},{16,18},{17,... | collective-permute-start | bytes 872 | tf_op jit(solution)/shard_map/ppermute | solution.py:14
  155.5 1.3 collective-permute-start.30
  156.8 1.3 collective-permute-start.18
  158.1 4.8 %collective-permute-start.19 = (f32[4,1,256]{2,0,1:T(4,128)S(1)}, f32[4,1,256]{2,0,1:T(4,128)S(1)}, u32[]{:S(2)}, u32[]{:S(2)}) collective-permute-start(f32[4,1,256]{2,0,1:T(4,128)S(1)} %get-tuple-element.140), channel_id=1, source_target_pairs={{0,4},{4,8},{8,12},{1,5},{5,9},{9,13},{2,6},{6,10},{10,14},{3,7},{... | collective-permute-start | bytes 12296 | tf_op jit(solution)/shard_map/ppermute | solution.py:14
  163.1 1.3 collective-permute-start.32
  164.4 4.6 %collective-permute-start.33 = (f32[4,1,128]{2,1,0:T(1,128)S(1)}, f32[4,1,128]{2,1,0:T(1,128)S(1)}, u32[]{:S(2)}, u32[]{:S(2)}) collective-permute-start(f32[4,1,128]{2,1,0:T(1,128)S(1)} %get-tuple-element.156), channel_id=1, source_target_pairs={{0,4},{4,8},{8,12},{1,5},{5,9},{9,13},{2,6},{6,10},{10,14},{3,7},{... | collective-permute-start | bytes 6152 | tf_op jit(solution)/shard_map/ppermute | solution.py:14
  169.0 0.8 gather_fusion.1
  169.8 15.5 %fusion = f32[4,128,128]{2,0,1:T(4,128)S(1)} fusion(f32[128,128,128]{2,1,0:T(8,128)} %param.30, f32[128,4,128]{2,1,0:T(4,128)S(1)} %gather_fusion.1, f32[128,128]{1,0:T(8,128)S(1)} %broadcast_multiply_fusion, pred[128]{0:T(512)(128)(4,1)S(1)} %compare_and_fusion), kind=kOutput, calls=%fused_computation.3 | convolution fusion | flops 100794368 | bytes 8978560 | tf_op jit(solution)/shard_map/bij,pbj->pbi/dot_general | solution.py:92
  185.3 9.4 %fusion.93 = f32[128,4,128]{2,1,0:T(4,128)S(1)} fusion(f32[4,128,128]{2,0,1:T(4,128)S(1)} %fusion, f32[128,128,128]{2,1,0:T(8,128)} %param.30), kind=kOutput, calls=%fused_computation.210 | convolution fusion | flops 100663296 | bytes 8912896 | tf_op jit(solution)/shard_map/bij,pbi->pbj/dot_general | solution.py:100
  195.2 3.9 %collective-permute-start.28 = (f32[4,384]{1,0:T(4,128)S(1)}, f32[4,384]{1,0:T(4,128)S(1)}, u32[]{:S(2)}, u32[]{:S(2)}) collective-permute-start(f32[4,384]{1,0:T(4,128)S(1)} %pad_maximum_fusion.76), channel_id=1, source_target_pairs={{0,4},{4,8},{8,12},{1,5},{5,9},{9,13},{2,6},{6,10},{10,14},{3,7},{... | collective-permute-start | bytes 18440 | tf_op jit(solution)/shard_map/ppermute | solution.py:25
  199.1 4.6 %collective-permute-start.21 = (f32[4,34,1]{2,0,1:T(4,128)S(1)}, f32[4,34,1]{2,0,1:T(4,128)S(1)}, u32[]{:S(2)}, u32[]{:S(2)}) collective-permute-start(f32[4,34,1]{2,0,1:T(4,128)S(1)} %get-tuple-element.129), channel_id=1, source_target_pairs={{0,2},{1,3},{4,6},{5,7},{8,10},{9,11},{12,14},{13,15},{16,18},{17,... | collective-permute-start | bytes 1640 | tf_op jit(solution)/shard_map/ppermute | solution.py:14
  203.7 1.3 collective-permute-start.20
  205.6 4.3 %collective-permute-done.20 = f32[4,34,1]{2,0,1:T(4,128)S(1)} collective-permute-done((f32[4,34,1]{2,0,1:T(4,128)S(1)}, f32[4,34,1]{2,0,1:T(4,128)S(1)}, u32[]{:S(2)}, u32[]{:S(2)}) %collective-permute-start.20) | collective-permute-done | bytes 576 | tf_op jit(solution)/shard_map/ppermute | solution.py:17
  210.1 1.3 collective-permute-start.22
  211.4 4.5 %collective-permute-start.23 = (f32[4,1,256]{2,0,1:T(4,128)S(1)}, f32[4,1,256]{2,0,1:T(4,128)S(1)}, u32[]{:S(2)}, u32[]{:S(2)}) collective-permute-start(f32[4,1,256]{2,0,1:T(4,128)S(1)} %get-tuple-element.138), channel_id=1, source_target_pairs={{0,4},{4,8},{8,12},{1,5},{5,9},{9,13},{2,6},{6,10},{10,14},{3,7},{... | collective-permute-start | bytes 12296 | tf_op jit(solution)/shard_map/ppermute | solution.py:14
  216.1 1.6 collective-permute-start.35
  217.6 1.3 collective-permute-start.34
  219.1 4.5 %collective-permute-start.25 = (f32[4,34,1]{2,0,1:T(4,128)S(1)}, f32[4,34,1]{2,0,1:T(4,128)S(1)}, u32[]{:S(2)}, u32[]{:S(2)}) collective-permute-start(f32[4,34,1]{2,0,1:T(4,128)S(1)} %get-tuple-element.127), channel_id=1, source_target_pairs={{0,2},{1,3},{4,6},{5,7},{8,10},{9,11},{12,14},{13,15},{16,18},{17,... | collective-permute-start | bytes 1640 | tf_op jit(solution)/shard_map/ppermute | solution.py:14
  223.6 1.3 collective-permute-start.24
  225.0 1.3 collective-permute-start.29
  226.3 4.2 %collective-permute-done.29 = f32[4,384]{1,0:T(4,128)S(1)} collective-permute-done((f32[4,384]{1,0:T(4,128)S(1)}, f32[4,384]{1,0:T(4,128)S(1)}, u32[]{:S(2)}, u32[]{:S(2)}) %collective-permute-start.29) | collective-permute-done | bytes 6176 | tf_op jit(solution)/shard_map/ppermute | solution.py:25
  231.2 5.5 %psum.46 = f32[4]{0:T(128)S(1)} all-reduce(f32[4]{0:T(128)S(1)} %add.239), channel_id=1, replica_groups=mesh['grp'=2,'ew'=4,'ns'=2,'lvl'=2] {'ns'}, use_global_device_ids=true, to_apply=%region_12.14 | all-reduce | flops 4 | bytes 32 | tf_op jit(solution)/shard_map/psum | solution.py:125
  236.7 8.4 %psum.47 = f32[4]{0:T(128)S(1)} all-reduce(f32[4]{0:T(128)S(1)} %psum.46), channel_id=1, replica_groups=mesh['grp'=2,'ew'=4,'ns'=2,'lvl'=2] {'ew'}, use_global_device_ids=true, to_apply=%region_13.15 | all-reduce | flops 4 | bytes 32 | tf_op jit(solution)/shard_map/psum | solution.py:124
  245.2 0.7 copy.51
  245.9 0.7 multiply_subtract_fusion.2
  246.6 0.7 copy.52
  (125 shorter events, 6.2 us)
Async XLA Ops:
  1.4 18.1 %collective-permute-start.9 = (f32[4,1,128]{2,1,0:T(1,128)S(1)}, f32[4,1,128]{2,1,0:T(1,128)S(1)}, u32[]{:S(2)}, u32[]{:S(2)}) collective-permute-start(f32[4,1,128]{2,1,0:T(1,128)S(1)} %get-tuple-element.163), channel_id=1, source_target_pairs={{4,0},{8,4},{12,8},{5,1},{9,5},{13,9},{6,2},{10,6},{14,10},{7,3},{... | collective-permute-start | bytes 6152 | tf_op jit(solution)/shard_map/ppermute | solution.py:17
  2.7 16.8 %collective-permute-start.8 = (f32[4,1,128]{2,1,0:T(1,128)S(1)}, f32[4,1,128]{2,1,0:T(1,128)S(1)}, u32[]{:S(2)}, u32[]{:S(2)}) collective-permute-start(f32[4,1,128]{2,1,0:T(1,128)S(1)} %get-tuple-element.162), channel_id=1, source_target_pairs={{0,4},{4,8},{8,12},{1,5},{5,9},{9,13},{2,6},{6,10},{10,14},{3,7},{... | collective-permute-start | bytes 6152 | tf_op jit(solution)/shard_map/ppermute | solution.py:14
  9.3 26.1 %collective-permute-start = (f32[4,1,256]{2,0,1:T(4,128)S(1)}, f32[4,1,256]{2,0,1:T(4,128)S(1)}, u32[]{:S(2)}, u32[]{:S(2)}) collective-permute-start(f32[4,1,256]{2,0,1:T(4,128)S(1)} %get-tuple-element.145), channel_id=1, source_target_pairs={{4,0},{8,4},{12,8},{5,1},{9,5},{13,9},{6,2},{10,6},{14,10},{7,3},{... | collective-permute-start | bytes 12296 | tf_op jit(solution)/shard_map/ppermute | solution.py:17
  10.6 24.8 %collective-permute-start.1 = (f32[4,1,256]{2,0,1:T(4,128)S(1)}, f32[4,1,256]{2,0,1:T(4,128)S(1)}, u32[]{:S(2)}, u32[]{:S(2)}) collective-permute-start(f32[4,1,256]{2,0,1:T(4,128)S(1)} %get-tuple-element.144), channel_id=1, source_target_pairs={{0,4},{4,8},{8,12},{1,5},{5,9},{9,13},{2,6},{6,10},{10,14},{3,7},{... | collective-permute-start | bytes 12296 | tf_op jit(solution)/shard_map/ppermute | solution.py:14
  19.6 5.6 %collective-permute-start.13 = (f32[4,18,1]{2,1,0:T(8,128)S(1)}, f32[4,18,1]{2,1,0:T(8,128)S(1)}, u32[]{:S(2)}, u32[]{:S(2)}) collective-permute-start(f32[4,18,1]{2,1,0:T(8,128)S(1)} %get-tuple-element.153), channel_id=1, source_target_pairs={{0,2},{1,3},{4,6},{5,7},{8,10},{9,11},{12,14},{13,15},{16,18},{17,... | collective-permute-start | bytes 872 | tf_op jit(solution)/shard_map/ppermute | solution.py:14
  23.5 6.0 %collective-permute-start.12 = (f32[4,18,1]{2,1,0:T(8,128)S(1)}, f32[4,18,1]{2,1,0:T(8,128)S(1)}, u32[]{:S(2)}, u32[]{:S(2)}) collective-permute-start(f32[4,18,1]{2,1,0:T(8,128)S(1)} %get-tuple-element.152), channel_id=1, source_target_pairs={{2,0},{3,1},{6,4},{7,5},{10,8},{11,9},{14,12},{15,13},{18,16},{19,... | collective-permute-start | bytes 872 | tf_op jit(solution)/shard_map/ppermute | solution.py:17
  29.6 37.6 %collective-permute-start.14 = (f32[4,1,128]{2,1,0:T(1,128)S(1)}, f32[4,1,128]{2,1,0:T(1,128)S(1)}, u32[]{:S(2)}, u32[]{:S(2)}) collective-permute-start(f32[4,1,128]{2,1,0:T(1,128)S(1)} %get-tuple-element.161), channel_id=1, source_target_pairs={{4,0},{8,4},{12,8},{5,1},{9,5},{13,9},{6,2},{10,6},{14,10},{7,3},{... | collective-permute-start | bytes 6152 | tf_op jit(solution)/shard_map/ppermute | solution.py:17
  30.9 36.4 %collective-permute-start.15 = (f32[4,1,128]{2,1,0:T(1,128)S(1)}, f32[4,1,128]{2,1,0:T(1,128)S(1)}, u32[]{:S(2)}, u32[]{:S(2)}) collective-permute-start(f32[4,1,128]{2,1,0:T(1,128)S(1)} %get-tuple-element.160), channel_id=1, source_target_pairs={{0,4},{4,8},{8,12},{1,5},{5,9},{9,13},{2,6},{6,10},{10,14},{3,7},{... | collective-permute-start | bytes 6152 | tf_op jit(solution)/shard_map/ppermute | solution.py:14
  36.3 16.4 %copy-start = (f32[128,128,128]{2,1,0:T(8,128)S(1)}, f32[128,128,128]{2,1,0:T(8,128)}, u32[]{:S(2)}) copy-start(f32[128,128,128]{2,1,0:T(8,128)} %param.30) | copy-start | bytes 25165828
  36.3 23.7 %copy-start.3 = (s32[128]{0:T(128)S(1)}, s32[128]{0:T(128)}, u32[]{:S(2)}) copy-start(s32[128]{0:T(128)} %param.32) | copy-start | bytes 1540
  36.3 56.5 %copy-start.1 = (s32[4,32,256]{2,1,0:T(8,128)S(1)}, s32[4,32,256]{2,1,0:T(8,128)}, u32[]{:S(2)}) copy-start(s32[4,32,256]{2,1,0:T(8,128)} %param.26) | copy-start | bytes 393220
  52.7 40.5 %copy-start.2 = (s32[4,16,128]{2,1,0:T(8,128)S(1)}, s32[4,16,128]{2,1,0:T(8,128)}, u32[]{:S(2)}) copy-start(s32[4,16,128]{2,1,0:T(8,128)} %param.27) | copy-start | bytes 98308
  60.6 26.6 %collective-permute-start.10 = (f32[4,384]{1,0:T(4,128)S(1)}, f32[4,384]{1,0:T(4,128)S(1)}, u32[]{:S(2)}, u32[]{:S(2)}) collective-permute-start(f32[4,384]{1,0:T(4,128)S(1)} %pad_maximum_fusion.74), channel_id=1, source_target_pairs={{0,4},{4,8},{8,12},{1,5},{5,9},{9,13},{2,6},{6,10},{10,14},{3,7},{... | collective-permute-start | bytes 18440 | tf_op jit(solution)/shard_map/ppermute | solution.py:25
  64.1 3.5 %collective-permute-start.3 = (f32[4,34,1]{2,0,1:T(4,128)S(1)}, f32[4,34,1]{2,0,1:T(4,128)S(1)}, u32[]{:S(2)}, u32[]{:S(2)}) collective-permute-start(f32[4,34,1]{2,0,1:T(4,128)S(1)} %get-tuple-element.135), channel_id=1, source_target_pairs={{0,2},{1,3},{4,6},{5,7},{8,10},{9,11},{12,14},{13,15},{16,18},{17,... | collective-permute-start | bytes 1640 | tf_op jit(solution)/shard_map/ppermute | solution.py:14
  65.7 6.4 %collective-permute-start.2 = (f32[4,34,1]{2,0,1:T(4,128)S(1)}, f32[4,34,1]{2,0,1:T(4,128)S(1)}, u32[]{:S(2)}, u32[]{:S(2)}) collective-permute-start(f32[4,34,1]{2,0,1:T(4,128)S(1)} %get-tuple-element.134), channel_id=1, source_target_pairs={{2,0},{3,1},{6,4},{7,5},{10,8},{11,9},{14,12},{15,13},{18,16},{19,... | collective-permute-start | bytes 1640 | tf_op jit(solution)/shard_map/ppermute | solution.py:17
  72.4 8.8 %collective-permute-start.4 = (f32[4,1,256]{2,0,1:T(4,128)S(1)}, f32[4,1,256]{2,0,1:T(4,128)S(1)}, u32[]{:S(2)}, u32[]{:S(2)}) collective-permute-start(f32[4,1,256]{2,0,1:T(4,128)S(1)} %get-tuple-element.143), channel_id=1, source_target_pairs={{4,0},{8,4},{12,8},{5,1},{9,5},{13,9},{6,2},{10,6},{14,10},{7,3},{... | collective-permute-start | bytes 12296 | tf_op jit(solution)/shard_map/ppermute | solution.py:17
  73.7 7.5 %collective-permute-start.5 = (f32[4,1,256]{2,0,1:T(4,128)S(1)}, f32[4,1,256]{2,0,1:T(4,128)S(1)}, u32[]{:S(2)}, u32[]{:S(2)}) collective-permute-start(f32[4,1,256]{2,0,1:T(4,128)S(1)} %get-tuple-element.142), channel_id=1, source_target_pairs={{0,4},{4,8},{8,12},{1,5},{5,9},{9,13},{2,6},{6,10},{10,14},{3,7},{... | collective-permute-start | bytes 12296 | tf_op jit(solution)/shard_map/ppermute | solution.py:14
  78.3 14.9 %collective-permute-start.17 = (f32[4,18,1]{2,1,0:T(8,128)S(1)}, f32[4,18,1]{2,1,0:T(8,128)S(1)}, u32[]{:S(2)}, u32[]{:S(2)}) collective-permute-start(f32[4,18,1]{2,1,0:T(8,128)S(1)} %get-tuple-element.151), channel_id=1, source_target_pairs={{0,2},{1,3},{4,6},{5,7},{8,10},{9,11},{12,14},{13,15},{16,18},{17,... | collective-permute-start | bytes 872 | tf_op jit(solution)/shard_map/ppermute | solution.py:14
  79.9 13.4 %collective-permute-start.16 = (f32[4,18,1]{2,1,0:T(8,128)S(1)}, f32[4,18,1]{2,1,0:T(8,128)S(1)}, u32[]{:S(2)}, u32[]{:S(2)}) collective-permute-start(f32[4,18,1]{2,1,0:T(8,128)S(1)} %get-tuple-element.150), channel_id=1, source_target_pairs={{2,0},{3,1},{6,4},{7,5},{10,8},{11,9},{14,12},{15,13},{18,16},{19,... | collective-permute-start | bytes 872 | tf_op jit(solution)/shard_map/ppermute | solution.py:17
  81.3 11.4 %collective-permute-start.7 = (f32[4,34,1]{2,0,1:T(4,128)S(1)}, f32[4,34,1]{2,0,1:T(4,128)S(1)}, u32[]{:S(2)}, u32[]{:S(2)}) collective-permute-start(f32[4,34,1]{2,0,1:T(4,128)S(1)} %get-tuple-element.133), channel_id=1, source_target_pairs={{0,2},{1,3},{4,6},{5,7},{8,10},{9,11},{12,14},{13,15},{16,18},{17,... | collective-permute-start | bytes 1640 | tf_op jit(solution)/shard_map/ppermute | solution.py:14
  85.9 6.9 %collective-permute-start.6 = (f32[4,34,1]{2,0,1:T(4,128)S(1)}, f32[4,34,1]{2,0,1:T(4,128)S(1)}, u32[]{:S(2)}, u32[]{:S(2)}) collective-permute-start(f32[4,34,1]{2,0,1:T(4,128)S(1)} %get-tuple-element.132), channel_id=1, source_target_pairs={{2,0},{3,1},{6,4},{7,5},{10,8},{11,9},{14,12},{15,13},{18,16},{19,... | collective-permute-start | bytes 1640 | tf_op jit(solution)/shard_map/ppermute | solution.py:17
  87.2 5.5 %collective-permute-start.11 = (f32[4,384]{1,0:T(4,128)S(1)}, f32[4,384]{1,0:T(4,128)S(1)}, u32[]{:S(2)}, u32[]{:S(2)}) collective-permute-start(f32[4,384]{1,0:T(4,128)S(1)} %pad_maximum_fusion.75), channel_id=1, source_target_pairs={{4,0},{8,4},{12,8},{5,1},{9,5},{13,9},{6,2},{10,6},{14,10},{7,3},{... | collective-permute-start | bytes 18440 | tf_op jit(solution)/shard_map/ppermute | solution.py:25
  145.8 5.9 %collective-permute-start.27 = (f32[4,1,128]{2,1,0:T(1,128)S(1)}, f32[4,1,128]{2,1,0:T(1,128)S(1)}, u32[]{:S(2)}, u32[]{:S(2)}) collective-permute-start(f32[4,1,128]{2,1,0:T(1,128)S(1)} %get-tuple-element.159), channel_id=1, source_target_pairs={{4,0},{8,4},{12,8},{5,1},{9,5},{13,9},{6,2},{10,6},{14,10},{7,3},{... | collective-permute-start | bytes 6152 | tf_op jit(solution)/shard_map/ppermute | solution.py:17
  147.1 5.8 %collective-permute-start.26 = (f32[4,1,128]{2,1,0:T(1,128)S(1)}, f32[4,1,128]{2,1,0:T(1,128)S(1)}, u32[]{:S(2)}, u32[]{:S(2)}) collective-permute-start(f32[4,1,128]{2,1,0:T(1,128)S(1)} %get-tuple-element.158), channel_id=1, source_target_pairs={{0,4},{4,8},{8,12},{1,5},{5,9},{9,13},{2,6},{6,10},{10,14},{3,7},{... | collective-permute-start | bytes 6152 | tf_op jit(solution)/shard_map/ppermute | solution.py:14
  153.0 9.9 %collective-permute-start.31 = (f32[4,18,1]{2,1,0:T(8,128)S(1)}, f32[4,18,1]{2,1,0:T(8,128)S(1)}, u32[]{:S(2)}, u32[]{:S(2)}) collective-permute-start(f32[4,18,1]{2,1,0:T(8,128)S(1)} %get-tuple-element.149), channel_id=1, source_target_pairs={{0,2},{1,3},{4,6},{5,7},{8,10},{9,11},{12,14},{13,15},{16,18},{17,... | collective-permute-start | bytes 872 | tf_op jit(solution)/shard_map/ppermute | solution.py:14
  155.5 7.4 %collective-permute-start.30 = (f32[4,18,1]{2,1,0:T(8,128)S(1)}, f32[4,18,1]{2,1,0:T(8,128)S(1)}, u32[]{:S(2)}, u32[]{:S(2)}) collective-permute-start(f32[4,18,1]{2,1,0:T(8,128)S(1)} %get-tuple-element.148), channel_id=1, source_target_pairs={{2,0},{3,1},{6,4},{7,5},{10,8},{11,9},{14,12},{15,13},{18,16},{19,... | collective-permute-start | bytes 872 | tf_op jit(solution)/shard_map/ppermute | solution.py:17
  156.8 12.1 %collective-permute-start.18 = (f32[4,1,256]{2,0,1:T(4,128)S(1)}, f32[4,1,256]{2,0,1:T(4,128)S(1)}, u32[]{:S(2)}, u32[]{:S(2)}) collective-permute-start(f32[4,1,256]{2,0,1:T(4,128)S(1)} %get-tuple-element.141), channel_id=1, source_target_pairs={{4,0},{8,4},{12,8},{5,1},{9,5},{13,9},{6,2},{10,6},{14,10},{7,3},{... | collective-permute-start | bytes 12296 | tf_op jit(solution)/shard_map/ppermute | solution.py:17
  158.1 10.8 %collective-permute-start.19 = (f32[4,1,256]{2,0,1:T(4,128)S(1)}, f32[4,1,256]{2,0,1:T(4,128)S(1)}, u32[]{:S(2)}, u32[]{:S(2)}) collective-permute-start(f32[4,1,256]{2,0,1:T(4,128)S(1)} %get-tuple-element.140), channel_id=1, source_target_pairs={{0,4},{4,8},{8,12},{1,5},{5,9},{9,13},{2,6},{6,10},{10,14},{3,7},{... | collective-permute-start | bytes 12296 | tf_op jit(solution)/shard_map/ppermute | solution.py:14
  163.1 41.9 %collective-permute-start.32 = (f32[4,1,128]{2,1,0:T(1,128)S(1)}, f32[4,1,128]{2,1,0:T(1,128)S(1)}, u32[]{:S(2)}, u32[]{:S(2)}) collective-permute-start(f32[4,1,128]{2,1,0:T(1,128)S(1)} %get-tuple-element.157), channel_id=1, source_target_pairs={{4,0},{8,4},{12,8},{5,1},{9,5},{13,9},{6,2},{10,6},{14,10},{7,3},{... | collective-permute-start | bytes 6152 | tf_op jit(solution)/shard_map/ppermute | solution.py:17
  164.4 40.6 %collective-permute-start.33 = (f32[4,1,128]{2,1,0:T(1,128)S(1)}, f32[4,1,128]{2,1,0:T(1,128)S(1)}, u32[]{:S(2)}, u32[]{:S(2)}) collective-permute-start(f32[4,1,128]{2,1,0:T(1,128)S(1)} %get-tuple-element.156), channel_id=1, source_target_pairs={{0,4},{4,8},{8,12},{1,5},{5,9},{9,13},{2,6},{6,10},{10,14},{3,7},{... | collective-permute-start | bytes 6152 | tf_op jit(solution)/shard_map/ppermute | solution.py:14
  195.2 29.8 %collective-permute-start.28 = (f32[4,384]{1,0:T(4,128)S(1)}, f32[4,384]{1,0:T(4,128)S(1)}, u32[]{:S(2)}, u32[]{:S(2)}) collective-permute-start(f32[4,384]{1,0:T(4,128)S(1)} %pad_maximum_fusion.76), channel_id=1, source_target_pairs={{0,4},{4,8},{8,12},{1,5},{5,9},{9,13},{2,6},{6,10},{10,14},{3,7},{... | collective-permute-start | bytes 18440 | tf_op jit(solution)/shard_map/ppermute | solution.py:25
  199.1 6.5 %collective-permute-start.21 = (f32[4,34,1]{2,0,1:T(4,128)S(1)}, f32[4,34,1]{2,0,1:T(4,128)S(1)}, u32[]{:S(2)}, u32[]{:S(2)}) collective-permute-start(f32[4,34,1]{2,0,1:T(4,128)S(1)} %get-tuple-element.129), channel_id=1, source_target_pairs={{0,2},{1,3},{4,6},{5,7},{8,10},{9,11},{12,14},{13,15},{16,18},{17,... | collective-permute-start | bytes 1640 | tf_op jit(solution)/shard_map/ppermute | solution.py:14
  203.7 6.2 %collective-permute-start.20 = (f32[4,34,1]{2,0,1:T(4,128)S(1)}, f32[4,34,1]{2,0,1:T(4,128)S(1)}, u32[]{:S(2)}, u32[]{:S(2)}) collective-permute-start(f32[4,34,1]{2,0,1:T(4,128)S(1)} %get-tuple-element.128), channel_id=1, source_target_pairs={{2,0},{3,1},{6,4},{7,5},{10,8},{11,9},{14,12},{15,13},{18,16},{19,... | collective-permute-start | bytes 1640 | tf_op jit(solution)/shard_map/ppermute | solution.py:17
  210.1 8.8 %collective-permute-start.22 = (f32[4,1,256]{2,0,1:T(4,128)S(1)}, f32[4,1,256]{2,0,1:T(4,128)S(1)}, u32[]{:S(2)}, u32[]{:S(2)}) collective-permute-start(f32[4,1,256]{2,0,1:T(4,128)S(1)} %get-tuple-element.139), channel_id=1, source_target_pairs={{4,0},{8,4},{12,8},{5,1},{9,5},{13,9},{6,2},{10,6},{14,10},{7,3},{... | collective-permute-start | bytes 12296 | tf_op jit(solution)/shard_map/ppermute | solution.py:17
  211.4 7.5 %collective-permute-start.23 = (f32[4,1,256]{2,0,1:T(4,128)S(1)}, f32[4,1,256]{2,0,1:T(4,128)S(1)}, u32[]{:S(2)}, u32[]{:S(2)}) collective-permute-start(f32[4,1,256]{2,0,1:T(4,128)S(1)} %get-tuple-element.138), channel_id=1, source_target_pairs={{0,4},{4,8},{8,12},{1,5},{5,9},{9,13},{2,6},{6,10},{10,14},{3,7},{... | collective-permute-start | bytes 12296 | tf_op jit(solution)/shard_map/ppermute | solution.py:14
  216.1 14.9 %collective-permute-start.35 = (f32[4,18,1]{2,1,0:T(8,128)S(1)}, f32[4,18,1]{2,1,0:T(8,128)S(1)}, u32[]{:S(2)}, u32[]{:S(2)}) collective-permute-start(f32[4,18,1]{2,1,0:T(8,128)S(1)} %get-tuple-element.147), channel_id=1, source_target_pairs={{0,2},{1,3},{4,6},{5,7},{8,10},{9,11},{12,14},{13,15},{16,18},{17,... | collective-permute-start | bytes 872 | tf_op jit(solution)/shard_map/ppermute | solution.py:14
  217.6 13.3 %collective-permute-start.34 = (f32[4,18,1]{2,1,0:T(8,128)S(1)}, f32[4,18,1]{2,1,0:T(8,128)S(1)}, u32[]{:S(2)}, u32[]{:S(2)}) collective-permute-start(f32[4,18,1]{2,1,0:T(8,128)S(1)} %get-tuple-element.146), channel_id=1, source_target_pairs={{2,0},{3,1},{6,4},{7,5},{10,8},{11,9},{14,12},{15,13},{18,16},{19,... | collective-permute-start | bytes 872 | tf_op jit(solution)/shard_map/ppermute | solution.py:17
  219.1 11.4 %collective-permute-start.25 = (f32[4,34,1]{2,0,1:T(4,128)S(1)}, f32[4,34,1]{2,0,1:T(4,128)S(1)}, u32[]{:S(2)}, u32[]{:S(2)}) collective-permute-start(f32[4,34,1]{2,0,1:T(4,128)S(1)} %get-tuple-element.127), channel_id=1, source_target_pairs={{0,2},{1,3},{4,6},{5,7},{8,10},{9,11},{12,14},{13,15},{16,18},{17,... | collective-permute-start | bytes 1640 | tf_op jit(solution)/shard_map/ppermute | solution.py:14
  223.6 6.9 %collective-permute-start.24 = (f32[4,34,1]{2,0,1:T(4,128)S(1)}, f32[4,34,1]{2,0,1:T(4,128)S(1)}, u32[]{:S(2)}, u32[]{:S(2)}) collective-permute-start(f32[4,34,1]{2,0,1:T(4,128)S(1)} %get-tuple-element.126), channel_id=1, source_target_pairs={{2,0},{3,1},{6,4},{7,5},{10,8},{11,9},{14,12},{15,13},{18,16},{19,... | collective-permute-start | bytes 1640 | tf_op jit(solution)/shard_map/ppermute | solution.py:17
  225.0 5.5 %collective-permute-start.29 = (f32[4,384]{1,0:T(4,128)S(1)}, f32[4,384]{1,0:T(4,128)S(1)}, u32[]{:S(2)}, u32[]{:S(2)}) collective-permute-start(f32[4,384]{1,0:T(4,128)S(1)} %pad_maximum_fusion.77), channel_id=1, source_target_pairs={{4,0},{8,4},{12,8},{5,1},{9,5},{13,9},{6,2},{10,6},{14,10},{7,3},{... | collective-permute-start | bytes 18440 | tf_op jit(solution)/shard_map/ppermute | solution.py:25
